TPU v7x, 512 devices: a whole 4x4x16 slice. The times are simulated.
512 devices in a mesh: fsdp: 32 (over z, core), expert: 16 (over x, y).
Axes of the slice: x: 4, y: 4, z: 16, core: 2. Of those that a mesh axis runs over, the one named last changes fastest.
Arguments:
- tokens: bfloat16 [65536, 4096], P(('fsdp', 'expert')), may hold values from -6 to 6
- expert_ids: int32 [65536, 2], P(('fsdp', 'expert')), may hold values from 0 to 15, all different within a row
- gate_probs: float32 [65536, 2], P(('fsdp', 'expert')), may hold values from 0.1 to 1
- up_weight: bfloat16 [16, 4096, 768], P('expert', 'fsdp'), may hold values from -0.09375 to 0.09375
- down_weight: bfloat16 [16, 768, 4096], P('expert', None, 'fsdp'), may hold values from -0.21875 to 0.21875
- out_grad: bfloat16 [65536, 4096], P(('fsdp', 'expert')), may hold values from -6 to 6
Outputs:
- d_tokens: bfloat16 [65536, 4096], P(('fsdp', 'expert'))
- d_gates: bfloat16 [65536, 2], P(('fsdp', 'expert'))
Inputs may be any that keep to these rules, and one draw needn't show every extreme that they name: `expert_ids`: each token names two different experts, and every expert is named by some token.
All inputs are finite; a program needn't handle non-finite values.
Results may differ from a plain program's by a relative error of at most 0.017.
Values may be sent and summed in bfloat16 or wider, within the bound.
No kernel may reach another device: no remote copies, remote signals or barrier semaphores. Data moves between devices by JAX's collectives and lax.ppermute only.
A program may use at most 64 MiB of HBM per device.

v0:
```python
import jax
import jax.numpy as jnp
from jax import lax
from jax.sharding import PartitionSpec as P


def gelu_parts(hidden):
    normal_cdf = 0.5 * (1.0 + lax.erf(hidden * 0.7071067811865476))
    density = jnp.exp(-0.5 * hidden * hidden) * 0.3989422804014327
    return (hidden * normal_cdf, normal_cdf + hidden * density)


def right_product(left, right):
    return lax.dot_general(
        left, right, (((1,), (1,)), ((), ())), preferred_element_type=jnp.float32
    )


def body(tokens, expert_ids, gate_probs, up_weight, down_weight, out_grad):
    experts = lax.axis_size("expert")
    token_count = tokens.shape[0]
    width = tokens.shape[1]
    capacity = 3 * token_count // (2 * experts)
    slot_count = experts * capacity
    flat_ids = expert_ids.reshape(-1)
    onehot = (flat_ids[:, None] == jnp.arange(experts, dtype=jnp.int32)[None, :]).astype(jnp.int32)
    position = jnp.sum((jnp.cumsum(onehot, axis=0) - 1) * onehot, axis=1)
    kept_mask = position < capacity
    slot_index = flat_ids * capacity + jnp.minimum(position, capacity - 1)
    target = jnp.where(kept_mask, slot_index, slot_count)
    match_rows = (jnp.arange(slot_count, dtype=jnp.int32)[:, None] == target[None, :]).astype(
        jnp.bfloat16
    )
    match_rows = match_rows.reshape(slot_count, token_count, 2).sum(axis=2)
    send_tokens = (
        jnp.dot(match_rows, tokens, preferred_element_type=jnp.float32)
        .astype(jnp.bfloat16)
        .reshape(experts, capacity, width)
    )
    send_grads = (
        jnp.dot(match_rows, out_grad, preferred_element_type=jnp.float32)
        .astype(jnp.bfloat16)
        .reshape(experts, capacity, width)
    )
    recv_tokens, recv_grads = (
        lax.all_to_all(send_tokens, "expert", split_axis=0, concat_axis=0, tiled=True),
        lax.all_to_all(send_grads, "expert", split_axis=0, concat_axis=0, tiled=True),
    )
    flat_tokens = recv_tokens.reshape(slot_count, width)
    up_full, down_full = (
        lax.all_gather(up_weight, "fsdp", axis=1, tiled=True),
        lax.all_gather(down_weight, "fsdp", axis=2, tiled=True),
    )
    up_matrix = up_full[0]
    hidden = jnp.dot(flat_tokens, up_matrix, preferred_element_type=jnp.float32)
    value, slope = gelu_parts(hidden)
    active = value.astype(jnp.bfloat16)
    flat_grads = recv_grads.reshape(slot_count, width)
    active_grad = right_product(flat_grads, down_full[0])
    gate_grad = jnp.sum(active.astype(jnp.float32) * active_grad, axis=1).astype(jnp.bfloat16)
    hidden_grad = (active_grad * slope).astype(jnp.bfloat16)
    input_grad = right_product(hidden_grad, up_matrix).astype(jnp.bfloat16)
    back_inputs, back_gates = (
        lax.all_to_all(
            input_grad.reshape(experts, capacity, width),
            "expert",
            split_axis=0,
            concat_axis=0,
            tiled=True,
        ),
        lax.all_to_all(
            gate_grad.reshape(experts, capacity), "expert", split_axis=0, concat_axis=0, tiled=True
        ),
    )
    picked = back_inputs.reshape(slot_count, width)[slot_index]
    weight = jnp.where(kept_mask, gate_probs.reshape(-1), 0.0)
    terms = (picked.astype(jnp.float32) * weight[:, None]).reshape(token_count, 2, width)
    d_tokens = (terms[:, 0, :] + terms[:, 1, :]).astype(jnp.bfloat16)
    d_gates = jnp.where(kept_mask, back_gates.reshape(-1)[slot_index], 0).reshape(token_count, 2)
    return (d_tokens, d_gates)


def solution(mesh):
    placed = (
        P(("fsdp", "expert"), None),
        P(("fsdp", "expert"), None),
        P(("fsdp", "expert"), None),
        P("expert", "fsdp", None),
        P("expert", None, "fsdp"),
        P(("fsdp", "expert"), None),
    )
    return jax.shard_map(
        body,
        mesh=mesh,
        in_specs=placed,
        out_specs=(P(("fsdp", "expert"), None), P(("fsdp", "expert"), None)),
        check_vma=False,
    )
```

profile of v0, /device:TPU:8, one launch (start us, length us, event | category | flops | bytes accessed | tf_op | source)
XLA Modules:
  0.0 259.5 jit_solution(20404745046377142)
XLA Ops:
  7.2 0.7 all-gather.5.cloned.1.call-update
  8.0 0.7 all-gather.3.cloned.1.call-update
  8.7 0.8 copy.27
  9.7 0.6 reduce-window.6
  10.3 0.2 slice_reduce_fusion
  11.1 0.6 convolution_convert_fusion
  11.7 1.5 reshape.144
  13.2 9.3 %all-to-all-start.1 = ((bf16[16,12,4096]{2,1,0:T(8,128)(2,1)}), bf16[16,12,4096]{2,1,0:T(8,128)(2,1)S(1)}, u32[]{:S(2)}, u32[]{:S(2)}) async-start(bf16[16,12,4096]{2,1,0:T(8,128)(2,1)} %reshape.144), calls=%async_computation.1 | async-start | bytes 4194304 | tf_op jit(solution)/shard_map/all_to_all | solution.py:46
  22.6 2.9 %convolution_convert_fusion.1 = bf16[192,4096]{1,0:T(8,128)(2,1)} fusion(bf16[192,128]{1,0:T(8,128)(2,1)S(1)} %fusion.21, bf16[128,4096]{1,0:T(8,128)(2,1)} %param.11), kind=kOutput, calls=%fused_computation.10 | convolution fusion | flops 202113024 | bytes 2670592 | tf_op jit(solution)/shard_map/dot_general | solution.py:41
  25.5 3.4 %reshape.142 = bf16[16,12,4096]{2,1,0:T(8,128)(2,1)} reshape(bf16[192,4096]{1,0:T(8,128)(2,1)} %convolution_convert_fusion.1) | data formatting | bytes 3145728 | tf_op jit(solution)/shard_map/reshape | solution.py:43
  28.9 20.3 %all-to-all-done.1 = bf16[16,12,4096]{2,1,0:T(8,128)(2,1)S(1)} async-done(((bf16[16,12,4096]{2,1,0:T(8,128)(2,1)}), bf16[16,12,4096]{2,1,0:T(8,128)(2,1)S(1)}, u32[]{:S(2)}, u32[]{:S(2)}) %all-to-all-start.1) | async-done | bytes 1572896 | tf_op jit(solution)/shard_map/all_to_all | solution.py:46
  49.2 5.6 %all-to-all-start = ((bf16[16,12,4096]{2,1,0:T(8,128)(2,1)}), bf16[16,12,4096]{2,1,0:T(8,128)(2,1)}, u32[]{:S(2)}, u32[]{:S(2)}) async-start(bf16[16,12,4096]{2,1,0:T(8,128)(2,1)} %reshape.142), calls=%async_computation | async-start | bytes 4194304 | tf_op jit(solution)/shard_map/all_to_all | solution.py:47
  54.8 1.4 reshape.145
  56.1 25.2 %all-to-all-done = bf16[16,12,4096]{2,1,0:T(8,128)(2,1)} async-done(((bf16[16,12,4096]{2,1,0:T(8,128)(2,1)}), bf16[16,12,4096]{2,1,0:T(8,128)(2,1)}, u32[]{:S(2)}, u32[]{:S(2)}) %all-to-all-start) | async-done | bytes 1572896 | tf_op jit(solution)/shard_map/all_to_all | solution.py:47
  81.3 2.5 reshape.143
  83.7 8.0 %all-gather.5.cloned.1.call-done = bf16[1,4096,768]{2,1,0:T(8,128)(2,1)} async-done(((bf16[1,128,768]{2,1,0:T(8,128)(2,1)}), bf16[1,4096,768]{2,1,0:T(8,128)(2,1)}) %all-gather.5.cloned.1.call-update) | async-done | bytes 6291472 | tf_op jit(solution)/shard_map/all_gather | solution.py:51
  91.7 4.7 %fusion.2 = f32[192,768]{1,0:T(8,128)S(1)} fusion(bf16[192,4096]{1,0:T(8,128)(2,1)} %reshape.145, bf16[1,4096,768]{2,1,0:T(8,128)(2,1)} %all-gather.5.cloned.1.call-done), kind=kOutput, calls=%fused_computation.4 | convolution fusion | flops 1207959552 | bytes 8454144 | tf_op jit(solution)/shard_map/dot_general | solution.py:55
  96.4 82.8 %all-gather.3.cloned.1.call-done = bf16[1,768,4096]{2,1,0:T(8,128)(2,1)} async-done(((bf16[1,768,128]{2,1,0:T(8,128)(2,1)}), bf16[1,768,4096]{2,1,0:T(8,128)(2,1)}) %all-gather.3.cloned.1.call-update) | async-done | bytes 6291472 | tf_op jit(solution)/shard_map/all_gather | solution.py:52
  179.1 5.8 %multiply_reduce_fusion = (bf16[192]{0:T(256)(128)(2,1)S(1)}, f32[192,768]{1,0:T(8,128)}) fusion(f32[192,768]{1,0:T(8,128)S(1)} %fusion.2, bf16[192,4096]{1,0:T(8,128)(2,1)S(1)} %reshape.143, bf16[1,768,4096]{2,1,0:T(8,128)(2,1)} %all-gather.3.cloned.1.call-done), kind=kOutput, calls=%fused_computation.22 | convolution fusion | flops 1209138944 | bytes 9044352 | tf_op jit(solution)/shard_map/dot_general | solution.py:14
  184.9 0.7 convert_element_type.73
  185.6 7.3 %all-to-all-start.3 = ((bf16[16,1,12]{2,1,0:T(2,128)(2,1)}), bf16[16,1,12]{2,1,0:T(2,128)(2,1)S(1)}, u32[]{:S(2)}, u32[]{:S(2)}) async-start(bf16[16,1,12]{2,1,0:T(2,128)(2,1)} %convert_element_type.73), calls=%async_computation.3 | async-start | bytes 16384 | tf_op jit(solution)/shard_map/all_to_all | solution.py:71
  192.9 5.1 %fusion.6 = bf16[192,4096]{1,0:T(8,128)(2,1)S(1)} fusion(bf16[1,4096,768]{2,1,0:T(8,128)(2,1)} %all-gather.5.cloned.1.call-done, f32[192,768]{1,0:T(8,128)} %get-tuple-element.11, f32[192,768]{1,0:T(8,128)S(1)} %fusion.2), kind=kOutput, calls=%fused_computation.8 | convolution fusion | flops 1210220544 | bytes 9043968 | tf_op jit(solution)/shard_map/dot_general | solution.py:14
  198.0 1.6 reshape.146
  199.6 7.4 %all-to-all-start.2 = ((bf16[16,12,4096]{2,1,0:T(8,128)(2,1)}), bf16[16,12,4096]{2,1,0:T(8,128)(2,1)}, u32[]{:S(2)}, u32[]{:S(2)}) async-start(bf16[16,12,4096]{2,1,0:T(8,128)(2,1)} %reshape.146), calls=%async_computation.2 | async-start | bytes 4194304 | tf_op jit(solution)/shard_map/all_to_all | solution.py:64
  207.5 1.9 gather_fusion.1
  209.5 0.6 copy.36
  210.1 25.7 %all-to-all-done.2 = bf16[16,12,4096]{2,1,0:T(8,128)(2,1)} async-done(((bf16[16,12,4096]{2,1,0:T(8,128)(2,1)}), bf16[16,12,4096]{2,1,0:T(8,128)(2,1)}, u32[]{:S(2)}, u32[]{:S(2)}) %all-to-all-start.2) | async-done | bytes 1572896 | tf_op jit(solution)/shard_map/all_to_all | solution.py:64
  235.8 2.5 reshape.147
  238.2 3.2 %gather_fusion = bf16[256,4096]{1,0:T(8,128)(2,1)} fusion(bf16[192,4096]{1,0:T(8,128)(2,1)S(1)} %reshape.147, s32[1024]{0:T(1024)S(1)} %pad_clamp_fusion), kind=kCustom, calls=%fused_computation | custom fusion | bytes 4195328 | tf_op jit(solution)/shard_map/gather | solution.py:75
  241.4 5.4 %reshape.149 = f32[128,2,4096]{2,1,0:T(2,128)} reshape(bf16[256,4096]{1,0:T(8,128)(2,1)} %gather_fusion) | data formatting | bytes 6291456 | tf_op jit(solution)/shard_map/convert_element_type | solution.py:77
  246.8 4.6 %copy_multiply_fusion = f32[128,2,4096]{2,0,1:T(8,128)S(1)} fusion(f32[128,2,4096]{2,1,0:T(2,128)} %reshape.149, f32[128,2]{0,1:T(2,128)S(1)} %copy.33), kind=kLoop, calls=%fused_computation.11 | loop fusion | flops 1048576 | bytes 8389632 | tf_op jit(solution)/shard_map/mul | solution.py:77
  251.5 1.2 fusion.10
  (30 shorter events, 1.6 us)
Async XLA Ops:
  7.2 4.0 %copy-start = (bf16[128,4096]{1,0:T(8,128)(2,1)S(1)}, bf16[128,4096]{1,0:T(8,128)(2,1)}, u32[]{:S(2)}) copy-start(bf16[128,4096]{1,0:T(8,128)(2,1)} %param.6) | copy-start | bytes 3145732
  7.2 84.5 %all-gather.5.cloned.1.call-start = ((), (), s32[]{:S(2)}) async-start(), calls=%async_computation.5 | async-start | bytes 6488064 | tf_op jit(solution)/shard_map/all_gather | solution.py:51
  7.9 171.2 %all-gather.3.cloned.1.call-start = ((), (), s32[]{:S(2)}) async-start(), calls=%async_computation.4 | async-start | bytes 6488064 | tf_op jit(solution)/shard_map/all_gather | solution.py:52
  13.2 35.9 %all-to-all-start.1 = ((bf16[16,12,4096]{2,1,0:T(8,128)(2,1)}), bf16[16,12,4096]{2,1,0:T(8,128)(2,1)S(1)}, u32[]{:S(2)}, u32[]{:S(2)}) async-start(bf16[16,12,4096]{2,1,0:T(8,128)(2,1)} %reshape.144), calls=%async_computation.1 | async-start | bytes 4194304 | tf_op jit(solution)/shard_map/all_to_all | solution.py:46
  49.2 32.1 %all-to-all-start = ((bf16[16,12,4096]{2,1,0:T(8,128)(2,1)}), bf16[16,12,4096]{2,1,0:T(8,128)(2,1)}, u32[]{:S(2)}, u32[]{:S(2)}) async-start(bf16[16,12,4096]{2,1,0:T(8,128)(2,1)} %reshape.142), calls=%async_computation | async-start | bytes 4194304 | tf_op jit(solution)/shard_map/all_to_all | solution.py:47
  185.6 14.0 %all-to-all-start.3 = ((bf16[16,1,12]{2,1,0:T(2,128)(2,1)}), bf16[16,1,12]{2,1,0:T(2,128)(2,1)S(1)}, u32[]{:S(2)}, u32[]{:S(2)}) async-start(bf16[16,1,12]{2,1,0:T(2,128)(2,1)} %convert_element_type.73), calls=%async_computation.3 | async-start | bytes 16384 | tf_op jit(solution)/shard_map/all_to_all | solution.py:71
  199.6 7.5 %copy-start.1 = (f32[128,2]{0,1:T(2,128)S(1)}, f32[128,2]{0,1:T(2,128)}, u32[]{:S(2)}) copy-start(f32[128,2]{0,1:T(2,128)} %param.8) | copy-start | bytes 3076
  199.6 36.2 %all-to-all-start.2 = ((bf16[16,12,4096]{2,1,0:T(8,128)(2,1)}), bf16[16,12,4096]{2,1,0:T(8,128)(2,1)}, u32[]{:S(2)}, u32[]{:S(2)}) async-start(bf16[16,12,4096]{2,1,0:T(8,128)(2,1)} %reshape.146), calls=%async_computation.2 | async-start | bytes 4194304 | tf_op jit(solution)/shard_map/all_to_all | solution.py:64
Sparse Core Ops, SparseCore 0:
  10.1 81.5 all-gather.4
  93.7 85.3 all-gather.2
where the time goes:
time: 260 us
  waiting for transfers between devices  163 us (63%)
  starting transfers between devices  29.6 us (11%)
  local copies, waits for them, and re-layouts  26.7 us (10%)
  matrix products  19.1 us (7%)
  between operations  14.2 us (5%)
  other arithmetic  6.7 us (3%)
    all_gather x1, waiting for transfers between devices, body(): lax.all_gather(down_weight, 'fsdp', axis=2, tiled=True)  82.8 us
    all_to_all x1, waiting for transfers between devices, body(): lax.all_to_all(input_grad.reshape(experts, capacity, width), 'expert', sp...  25.7 us
    all_to_all x1, waiting for transfers between devices, body(): lax.all_to_all(send_grads, 'expert', split_axis=0, concat_axis=0, tiled=T...  25.2 us
    all_to_all x1, waiting for transfers between devices, body(): lax.all_to_all(send_tokens, 'expert', split_axis=0, concat_axis=0, tiled=...  20.3 us
    dot_general x2, matrix products, right_product(): lax.dot_general(left, right, (((1,), (1,)), ((), ())), preferred_element_...  10.9 us
    all_to_all x1, starting transfers between devices, body(): lax.all_to_all(send_tokens, 'expert', split_axis=0, concat_axis=0, tiled=...  9.33 us
    all_gather x1, waiting for transfers between devices, body(): lax.all_gather(up_weight, 'fsdp', axis=1, tiled=True)  7.95 us
    all_to_all x1, starting transfers between devices, body(): lax.all_to_all(input_grad.reshape(experts, capacity, width), 'expert', sp...  7.35 us
  transfers between devices with their start and end apart: 6, of which 5 were waited for; matrix products, arithmetic and copies ran while one was open for 11% of the time, Pallas kernels for 0%

commit v1 on v0

--- a/solution.py
+++ b/solution.py
@@ -48,7 +48,9 @@
     )
     flat_tokens = recv_tokens.reshape(slot_count, width)
     up_full, down_full = (
-        lax.all_gather(up_weight, "fsdp", axis=1, tiled=True),
+        jnp.concatenate(
+            lax.all_to_all(jnp.stack([up_weight] * lax.axis_size("fsdp")), "fsdp", 0, 0), axis=1
+        ),
         lax.all_gather(down_weight, "fsdp", axis=2, tiled=True),
     )
     up_matrix = up_full[0]

time: 260 us -> 492 us (1.89)
  the two profiles are of different devices: /device:TPU:8 before, /device:TPU:32 now
where the time goes in v1:
time: 492 us
  waiting for transfers between devices  358 us (73%)
  starting transfers between devices  32.7 us (7%)
  blocking collectives  30.3 us (6%)
  local copies, waits for them, and re-layouts  30.2 us (6%)
  matrix products  19.1 us (4%)
  between operations  14.2 us (3%)
  other arithmetic  6.7 us (1%)
    all_to_all x1, waiting for transfers between devices, body(): lax.all_to_all(jnp.stack([up_weight] * lax.axis_size('fsdp')), 'fsdp', 0, 0)  307 us
    all_to_all x1, blocking collectives, body(): lax.all_to_all(send_grads, 'expert', split_axis=0, concat_axis=0, tiled=T...  30.3 us
    all_to_all x1, waiting for transfers between devices, body(): lax.all_to_all(input_grad.reshape(experts, capacity, width), 'expert', sp...  25.8 us
    all_to_all x1, waiting for transfers between devices, body(): lax.all_to_all(send_tokens, 'expert', split_axis=0, concat_axis=0, tiled=...  24 us
    all_to_all x1, starting transfers between devices, body(): lax.all_to_all(jnp.stack([up_weight] * lax.axis_size('fsdp')), 'fsdp', 0, 0)  15.4 us
    dot_general x2, matrix products, right_product(): lax.dot_general(left, right, (((1,), (1,)), ((), ())), preferred_element_...  10.9 us
  transfers between devices with their start and end apart: 5, of which 4 were waited for; matrix products, arithmetic and copies ran while one was open for 5% of the time, Pallas kernels for 0%

profile of v1, /device:TPU:32, one launch (start us, length us, event | category | flops | bytes accessed | tf_op | source)
XLA Modules:
  0.0 491.6 jit_solution(514194622003335645)
XLA Ops:
  7.2 0.9 copy.27
  8.3 0.6 reduce-window.6
  8.9 0.2 slice_reduce_fusion
  9.7 0.6 convolution_convert_fusion.1
  10.3 1.6 reshape.147
  11.8 7.0 %all-to-all-start.1 = ((bf16[16,12,4096]{2,1,0:T(8,128)(2,1)}), bf16[16,12,4096]{2,1,0:T(8,128)(2,1)S(1)}, u32[]{:S(2)}, u32[]{:S(2)}) async-start(bf16[16,12,4096]{2,1,0:T(8,128)(2,1)} %reshape.147), calls=%async_computation.1 | async-start | bytes 4194304 | tf_op jit(solution)/shard_map/all_to_all | solution.py:46
  18.9 3.0 convolution_convert_fusion.2
  21.8 3.4 reshape.145
  25.3 24.0 %all-to-all-done.1 = bf16[16,12,4096]{2,1,0:T(8,128)(2,1)S(1)} async-done(((bf16[16,12,4096]{2,1,0:T(8,128)(2,1)}), bf16[16,12,4096]{2,1,0:T(8,128)(2,1)S(1)}, u32[]{:S(2)}, u32[]{:S(2)}) %all-to-all-start.1) | async-done | bytes 1572896 | tf_op jit(solution)/shard_map/all_to_all | solution.py:46
  49.3 30.3 %all_to_all.26 = bf16[16,12,4096]{2,1,0:T(8,128)(2,1)} all-to-all(bf16[16,12,4096]{2,1,0:T(8,128)(2,1)} %reshape.145), channel_id=1, replica_groups=mesh['fsdp'=32,'expert'=16] {'expert'}, dimensions={0} | all-to-all | bytes 3145728 | tf_op jit(solution)/shard_map/all_to_all | solution.py:47
  79.5 3.3 stack.2
  82.9 15.4 %all-to-all-start.2 = ((bf16[32,1,128,768]{3,2,1,0:T(8,128)(2,1)}), bf16[32,1,128,768]{3,2,1,0:T(8,128)(2,1)}, u32[]{:S(2)}, u32[]{:S(2)}) async-start(bf16[32,1,128,768]{3,2,1,0:T(8,128)(2,1)} %stack.2), calls=%async_computation.2 | async-start | bytes 12582912 | tf_op jit(solution)/shard_map/all_to_all | solution.py:52
  98.3 0.7 all-gather.2.cloned.1.call-update
  99.0 1.4 reshape.148
  100.4 2.5 reshape.146
  102.8 307.0 %all-to-all-done.2 = bf16[32,1,128,768]{3,2,1,0:T(8,128)(2,1)} async-done(((bf16[32,1,128,768]{3,2,1,0:T(8,128)(2,1)}), bf16[32,1,128,768]{3,2,1,0:T(8,128)(2,1)}, u32[]{:S(2)}, u32[]{:S(2)}) %all-to-all-start.2) | async-done | bytes 6291488 | tf_op jit(solution)/shard_map/all_to_all | solution.py:52
  409.8 4.7 fusion.20
  414.5 5.8 %multiply_reduce_fusion = (bf16[192]{0:T(256)(128)(2,1)S(1)}, f32[192,768]{1,0:T(8,128)}) fusion(f32[192,768]{1,0:T(8,128)S(1)} %fusion.20, bf16[192,4096]{1,0:T(8,128)(2,1)S(1)} %reshape.146, bf16[1,768,4096]{2,1,0:T(8,128)(2,1)} %all-gather.2.cloned.1.call-done), kind=kOutput, calls=%fused_computation.18 | convolution fusion | flops 1209138944 | bytes 9044352 | tf_op jit(solution)/shard_map/dot_general | solution.py:14
  420.3 0.7 convert_element_type.73
  421.0 3.7 all-to-all-start.4
  424.7 5.1 %convolution_convert_fusion = bf16[192,4096]{1,0:T(8,128)(2,1)S(1)} fusion(bf16[4096,768]{1,0:T(8,128)(2,1)} %bitcast.3, f32[192,768]{1,0:T(8,128)} %get-tuple-element.11, f32[192,768]{1,0:T(8,128)S(1)} %fusion.20), kind=kOutput, calls=%fused_computation.4 | convolution fusion | flops 1210220544 | bytes 9043968 | tf_op jit(solution)/shard_map/dot_general | solution.py:14
  429.8 1.6 reshape.149
  431.4 0.9 all-to-all-done.4
  432.2 6.6 %all-to-all-start.3 = ((bf16[16,12,4096]{2,1,0:T(8,128)(2,1)}), bf16[16,12,4096]{2,1,0:T(8,128)(2,1)}, u32[]{:S(2)}, u32[]{:S(2)}) async-start(bf16[16,12,4096]{2,1,0:T(8,128)(2,1)} %reshape.149), calls=%async_computation.3 | async-start | bytes 4194304 | tf_op jit(solution)/shard_map/all_to_all | solution.py:66
  439.3 1.9 gather_fusion.1
  441.4 0.6 copy.36
  442.0 25.8 %all-to-all-done.3 = bf16[16,12,4096]{2,1,0:T(8,128)(2,1)} async-done(((bf16[16,12,4096]{2,1,0:T(8,128)(2,1)}), bf16[16,12,4096]{2,1,0:T(8,128)(2,1)}, u32[]{:S(2)}, u32[]{:S(2)}) %all-to-all-start.3) | async-done | bytes 1572896 | tf_op jit(solution)/shard_map/all_to_all | solution.py:66
  467.8 2.5 reshape.150
  470.3 3.2 gather_fusion
  473.4 5.4 %reshape.152 = f32[128,2,4096]{2,1,0:T(2,128)} reshape(bf16[256,4096]{1,0:T(8,128)(2,1)} %gather_fusion) | data formatting | bytes 6291456 | tf_op jit(solution)/shard_map/convert_element_type | solution.py:79
  478.9 4.6 copy_multiply_fusion
  483.5 1.2 fusion.3
  (31 shorter events, 1.6 us)
Async XLA Ops:
  7.2 2.6 copy-start
  11.8 37.4 %all-to-all-start.1 = ((bf16[16,12,4096]{2,1,0:T(8,128)(2,1)}), bf16[16,12,4096]{2,1,0:T(8,128)(2,1)S(1)}, u32[]{:S(2)}, u32[]{:S(2)}) async-start(bf16[16,12,4096]{2,1,0:T(8,128)(2,1)} %reshape.147), calls=%async_computation.1 | async-start | bytes 4194304 | tf_op jit(solution)/shard_map/all_to_all | solution.py:46
  25.3 54.3 %copy-start.1 = (bf16[1,128,768]{2,1,0:T(8,128)(2,1)S(1)}, bf16[1,128,768]{2,1,0:T(8,128)(2,1)}, u32[]{:S(2)}) copy-start(bf16[1,128,768]{2,1,0:T(8,128)(2,1)} %param.9) | copy-start | bytes 589828
  82.9 327.0 %all-to-all-start.2 = ((bf16[32,1,128,768]{3,2,1,0:T(8,128)(2,1)}), bf16[32,1,128,768]{3,2,1,0:T(8,128)(2,1)}, u32[]{:S(2)}, u32[]{:S(2)}) async-start(bf16[32,1,128,768]{3,2,1,0:T(8,128)(2,1)} %stack.2), calls=%async_computation.2 | async-start | bytes 12582912 | tf_op jit(solution)/shard_map/all_to_all | solution.py:52
  98.3 316.2 %all-gather.2.cloned.1.call-start = ((), (), s32[]{:S(2)}) async-start(), calls=%async_computation.5 | async-start | bytes 6488064 | tf_op jit(solution)/shard_map/all_gather | solution.py:54
  421.0 11.2 %all-to-all-start.4 = ((bf16[16,1,12]{2,1,0:T(2,128)(2,1)}), bf16[16,1,12]{2,1,0:T(2,128)(2,1)S(1)}, u32[]{:S(2)}, u32[]{:S(2)}) async-start(bf16[16,1,12]{2,1,0:T(2,128)(2,1)} %convert_element_type.73), calls=%async_computation.4 | async-start | bytes 16384 | tf_op jit(solution)/shard_map/all_to_all | solution.py:73
  431.4 7.6 %copy-start.2 = (f32[128,2]{0,1:T(2,128)S(1)}, f32[128,2]{0,1:T(2,128)}, u32[]{:S(2)}) copy-start(f32[128,2]{0,1:T(2,128)} %param.8) | copy-start | bytes 3076
  432.2 35.6 %all-to-all-start.3 = ((bf16[16,12,4096]{2,1,0:T(8,128)(2,1)}), bf16[16,12,4096]{2,1,0:T(8,128)(2,1)}, u32[]{:S(2)}, u32[]{:S(2)}) async-start(bf16[16,12,4096]{2,1,0:T(8,128)(2,1)} %reshape.149), calls=%async_computation.3 | async-start | bytes 4194304 | tf_op jit(solution)/shard_map/all_to_all | solution.py:66
Sparse Core Ops, SparseCore 0:
  101.2 281.8 all-gather.1
